TPU v7x, 32 devices: a whole 2x2x4 slice. The times are simulated.
32 devices in a mesh: axial: 4 (over y, core), azim: 8 (over z, x).
Axes of the slice: x: 2, y: 2, z: 4, core: 2. Of those that a mesh axis runs over, the one named last changes fastest.
Arguments:
- state: float32 [5, 64, 131072], P(None, 'axial', 'azim'), may hold values from -6 to 6
- profile: float32 [64, 131072], P(None, ('axial', 'azim')), may hold values from -6 to 6
- samp_cell: int32 [32, 32, 128], P(('axial', 'azim')), may hold values from 0 to 262143
- own_live: int32 [32], replicated, may hold values from 1 to 4096, 65536 in all
Outputs:
- new_profile: float32 [64, 131072], P(None, ('axial', 'azim'))
- wall_stress: float32 [2, 131072], P(None, ('axial', 'azim'))
Inputs may be any that keep to these rules, and one draw needn't show every extreme that they name: own_live sums to 32 * 4096 // 2 over all owners.
All inputs are finite; a program needn't handle non-finite values.
Results may differ from a plain program's by a relative error of at most 0.0003.
Values sent between devices are 32-bit elements; how exact they have to be, the bound alone decides.
A program may use at most 320 MiB of HBM per device.

v0:
```python
import jax
import jax.numpy as jnp
from jax import lax
from jax.sharding import PartitionSpec as P

ITERS = 3


def extended(block, sides, width):
    for axis, dim in sides:
        count = lax.axis_size(axis)
        forward = [(i, i + 1) for i in range(count - 1)]
        forward.append((count - 1, 0))
        backward = [(target, source) for source, target in forward]
        low = lax.ppermute(
            lax.slice_in_dim(block, block.shape[dim] - width, None, axis=dim), axis, forward
        )
        high = lax.ppermute(lax.slice_in_dim(block, 0, width, axis=dim), axis, backward)
        block = jnp.concatenate([low, block, high], axis=dim)
    return block


def thomas(lower_rows, diag_rows, upper_rows, rhs_rows):
    count = len(rhs_rows)
    zeros = jnp.zeros_like(rhs_rows[0])
    c_prev = zeros
    d_prev = zeros
    c_list = []
    d_list = []
    for row in range(count):
        denom = diag_rows[row] - lower_rows[row] * c_prev
        c_new = upper_rows[row] / denom
        d_new = (rhs_rows[row] - lower_rows[row] * d_prev) / denom
        c_list.append(c_new)
        d_list.append(d_new)
        c_prev = c_new
        d_prev = d_new
    after = zeros
    values = [zeros] * count
    for row in range(count - 1, -1, -1):
        after = d_list[row] - c_list[row] * after
        values[row] = after
    return jnp.stack(values, axis=0)


def wall_solve(profile, match):
    points = profile.shape[0]
    step = 1.0 / (points - 1)
    density = jnp.exp(0.3 * match[0])
    vel_ax = match[1]
    vel_az = match[2]
    source = 0.5 * match[3]
    visc = 0.01 * jnp.exp(0.5 * match[4])
    speed = jnp.sqrt(vel_ax * vel_ax + vel_az * vel_az + 0.25)
    mixing = 0.41 * (jnp.arange(points - 1, dtype=jnp.float32) + 0.5) * step
    mix_sq = (mixing * mixing)[:, None]
    zero_row = jnp.zeros_like(profile[0])
    one_row = jnp.ones_like(profile[0])
    velocity = profile
    for sweep in range(ITERS):
        grad = (velocity[1:] - velocity[:-1]) / step
        root = jnp.sqrt(grad * grad + 1.0)
        flux = (visc + mix_sq * root) * grad
        slope = visc + mix_sq * (root + grad * grad / root)
        inner = -(step * (flux[1:] - flux[:-1]) - source * step * step)
        lower_rows = [zero_row] + [slope[i - 1] for i in range(1, points - 1)] + [zero_row]
        upper_rows = [zero_row] + [slope[i] for i in range(1, points - 1)] + [zero_row]
        diag_rows = (
            [one_row] + [-(slope[i] + slope[i - 1]) for i in range(1, points - 1)] + [one_row]
        )
        rhs_rows = (
            [-velocity[0]] + [inner[i - 1] for i in range(1, points - 1)] + [speed - velocity[-1]]
        )
        velocity = velocity + thomas(lower_rows, diag_rows, upper_rows, rhs_rows)
    shear = density * visc * (velocity[1] - velocity[0]) / step
    stress = jnp.stack([shear * vel_ax / speed, shear * vel_az / speed], axis=0)
    return (velocity, stress)


def body(state, profile, samp_cell, own_live):
    comps, slab_rows, section = state.shape
    points, owned = profile.shape
    devices = lax.axis_size(("axial", "azim"))
    padded = extended(state, (("axial", 1),), 1)
    smoothed = 0.25 * padded[:, :-2, :] + 0.5 * padded[:, 1:-1, :] + 0.25 * padded[:, 2:, :]
    flat = smoothed.reshape(comps, slab_rows * section)
    cells = samp_cell.reshape(-1)
    filtered = flat[:, cells]
    outgoing = filtered.reshape(comps, devices, samp_cell.shape[2])
    arrived = lax.all_to_all(outgoing, ("axial", "azim"), split_axis=1, concat_axis=1, tiled=True)
    match = arrived.reshape(comps, owned)
    here = lax.axis_index(("axial", "azim"))
    slots = owned // devices
    share = owned // 2
    starts = jnp.cumsum(own_live) - own_live
    block_ids = jnp.arange(devices, dtype=jnp.int32)[:, None]
    slot_ids = jnp.arange(slots, dtype=jnp.int32)[None, :]
    send_rows = slot_ids * devices + (block_ids - starts[here]) % devices
    send_rows = jnp.minimum(send_rows, owned - 1).reshape(-1)
    send_prof = profile[:, send_rows].reshape(points, devices, slots)
    send_match = match[:, send_rows].reshape(comps, devices, slots)
    got_prof, got_match = (
        lax.all_to_all(send_prof, ("axial", "azim"), split_axis=1, concat_axis=1, tiled=True),
        lax.all_to_all(send_match, ("axial", "azim"), split_axis=1, concat_axis=1, tiled=True),
    )
    column = jnp.arange(share, dtype=jnp.int32) * devices + here
    owner_of = jnp.sum((starts[None, :] <= column[:, None]).astype(jnp.int32), axis=1) - 1
    within = column - starts[owner_of]
    pick = owner_of * slots + within // devices
    work_prof = got_prof.reshape(points, devices * slots)[:, pick]
    work_match = got_match.reshape(comps, devices * slots)[:, pick]
    done_prof, done_stress = wall_solve(work_prof, work_match)
    back_rows = slot_ids * devices + (here - starts[:, None]) % devices
    back_index = jnp.minimum((starts[:, None] + back_rows) // devices, share - 1).reshape(-1)
    ret_prof = done_prof[:, back_index].reshape(points, devices, slots)
    ret_stress = done_stress[:, back_index].reshape(2, devices, slots)
    back_prof, back_stress = (
        lax.all_to_all(ret_prof, ("axial", "azim"), split_axis=1, concat_axis=1, tiled=True),
        lax.all_to_all(ret_stress, ("axial", "azim"), split_axis=1, concat_axis=1, tiled=True),
    )
    own_rows = jnp.arange(owned, dtype=jnp.int32)
    home = (starts[here] + own_rows) % devices * slots + jnp.minimum(own_rows // devices, slots - 1)
    solved = back_prof.reshape(points, devices * slots)[:, home]
    stress = back_stress.reshape(2, devices * slots)[:, home]
    live_count = own_live[here]
    burning = jnp.arange(owned, dtype=jnp.int32)[None, :] < live_count
    new_profile = jnp.where(burning, solved, profile)
    wall_stress = jnp.where(burning, stress, jnp.float32(0.0))
    return (new_profile, wall_stress)


def solution(mesh):
    return jax.shard_map(
        body,
        mesh=mesh,
        in_specs=(
            P(None, "axial", "azim"),
            P(None, ("axial", "azim")),
            P(("axial", "azim"), None, None),
            P(),
        ),
        out_specs=(P(None, ("axial", "azim")), P(None, ("axial", "azim"))),
        check_vma=False,
    )
```

profile of v0, /device:TPU:0, one launch (start us, length us, event | category | flops | bytes accessed | tf_op | source)
XLA Modules:
  0.0 384.9 jit_solution(2192533032639424645)
XLA Ops:
  0.7 3.0 fusion.263
  8.6 4.4 %compare_select_fusion.11 = (s32[2048,1]{0,1:T(1,128)S(1)}, s32[2048,1]{0,1:T(1,128)S(1)}) fusion(s32[]{:T(128)} %bitcast.35, s32[]{:T(128)} %bitcast.36, s32[]{:T(128)} %bitcast.37, s32[]{:T(128)} %bitcast.38, s32[]{:T(128)} %bitcast.39, s32[]{:T(128)} %bitcast.41, s32[]{:T(128)} %bitcast.40, s32[2048,1]{0,1:T(1,128)S(1)} %bitcast.1336, ...), kind=kLoop, calls=%fused_computation.93 | loop fusion | flops 28672 | bytes 32796 | tf_op jit(solution)/shard_map/gather | solution.py:108
  13.0 2.9 collective-permute-done
  19.0 8.4 %fusion.1 = f32[5,16,16384]{2,1,0:T(8,128)} fusion(f32[5,1,16384]{2,1,0:T(1,128)S(1)} %copy.298, f32[5,16,16384]{2,1,0:T(8,128)} %param.4, f32[5,1,16384]{2,1,0:T(1,128)S(1)} %copy.296), kind=kLoop, calls=%fused_computation.11 | loop fusion | flops 9175040 | bytes 11141120 | tf_op jit(solution)/shard_map/add | solution.py:85
  27.4 61.0 %copy.299 = f32[5,16,16384]{0,2,1:T(8,128)} copy(f32[5,16,16384]{2,1,0:T(8,128)} %fusion.1) | data formatting | bytes 10485760 | tf_op jit(solution)/shard_map/add | solution.py:85
  88.4 40.3 %gather_fusion.2 = f32[4096,5]{1,0:T(8,128)S(1)} fusion(f32[5,262144]{0,1:T(8,128)} %bitcast.47, s32[4096]{0:T(1024)S(1)} %broadcast_clamp_fusion.1), kind=kCustom, calls=%fused_computation.2 | custom fusion | bytes 180224 | tf_op jit(solution)/shard_map/gather | solution.py:88
  130.0 6.3 %all-to-all-start.1 = ((f32[5,32,128]{2,0,1:T(8,128)}), f32[5,32,128]{2,0,1:T(8,128)S(1)}, u32[]{:S(2)}, u32[]{:S(2)}) async-start(f32[5,32,128]{2,0,1:T(8,128)} %copy.300), calls=%async_computation.1 | async-start | bytes 262144 | tf_op jit(solution)/shard_map/all_to_all | solution.py:90
  137.7 14.2 %gather_fusion = f32[4096,64]{1,0:T(8,128)} fusion(f32[64,4096]{0,1:T(8,128)S(1)} %copy.291, s32[4096]{0:T(1024)S(1)} %broadcast_clamp_fusion.3), kind=kCustom, calls=%fused_computation | custom fusion | bytes 2113536 | tf_op jit(solution)/shard_map/gather | solution.py:100
  151.9 3.1 copy.292
  157.6 15.8 %gather_fusion.3 = f32[4096,5]{1,0:T(8,128)} fusion(f32[5,4096]{0,1:T(8,128)} %bitcast.538, s32[4096]{0:T(1024)S(1)} %broadcast_clamp_fusion.3), kind=kCustom, calls=%fused_computation.3 | custom fusion | bytes 180224 | tf_op jit(solution)/shard_map/gather | solution.py:101
  173.4 2.9 copy.302
  176.2 5.8 %all-to-all-start.2 = ((f32[5,32,128]{2,0,1:T(8,128)}), f32[5,32,128]{2,0,1:T(8,128)S(1)}, u32[]{:S(2)}, u32[]{:S(2)}) async-start(f32[5,32,128]{2,0,1:T(8,128)} %copy.302), calls=%async_computation.2 | async-start | bytes 262144 | tf_op jit(solution)/shard_map/all_to_all | solution.py:104
  182.1 15.8 %select_select_fusion = s32[2048]{0:T(1024)S(1)} fusion(pred[2048]{0:T(1024)(128)(4,1)S(1)} %get-tuple-element.36, pred[2048]{0:T(1024)(128)(4,1)S(1)} %get-tuple-element.35, pred[2048]{0:T(1024)(128)(4,1)S(1)} %get-tuple-element.34, pred[2048]{0:T(1024)(128)(4,1)S(1)} %get-tuple-element.33, pred[2048]{0:T(1024)(128)(4,1)S(1)} %get-tuple-element.32, ...), kind=kLoop, calls=%fused_computation.142 | loop fusion | flops 51200 | bytes 67684 | tf_op jit(solution)/shard_map/gather | solution.py:108
  197.8 5.8 %all-to-all-start = ((f32[64,32,128]{2,0,1:T(8,128)}), f32[64,32,128]{2,0,1:T(8,128)S(1)}, u32[]{:S(2)}, u32[]{:S(2)}) async-start(f32[64,32,128]{2,0,1:T(8,128)} %copy.292), calls=%async_computation | async-start | bytes 2097152 | tf_op jit(solution)/shard_map/all_to_all | solution.py:103
  205.9 9.2 %gather_fusion.4 = f32[2048,5]{1,0:T(8,128)} fusion(f32[5,4096]{0,1:T(8,128)} %bitcast.539, s32[2048]{0:T(1024)S(1)} %broadcast_clamp_fusion.4), kind=kCustom, calls=%fused_computation.4 | custom fusion | bytes 90112 | tf_op jit(solution)/shard_map/gather | solution.py:111
  216.7 14.6 %all-to-all-done = f32[64,32,128]{2,0,1:T(8,128)S(1)} async-done(((f32[64,32,128]{2,0,1:T(8,128)}), f32[64,32,128]{2,0,1:T(8,128)S(1)}, u32[]{:S(2)}, u32[]{:S(2)}) %all-to-all-start) | async-done | bytes 1048608 | tf_op jit(solution)/shard_map/all_to_all | solution.py:103
  233.2 9.2 %gather_fusion.1 = f32[2048,64]{1,0:T(8,128)} fusion(f32[64,4096]{0,1:T(8,128)} %bitcast.531, s32[2048]{0:T(1024)S(1)} %broadcast_clamp_fusion.4), kind=kCustom, calls=%fused_computation.1 | custom fusion | bytes 1056768 | tf_op jit(solution)/shard_map/gather | solution.py:110
  250.3 5.8 %stack.176 = f32[64,2048]{1,0:T(8,128)} concatenate(f32[1,2048]{1,0:T(1,128)S(1)} %bitcast.1247, f32[1,2048]{1,0:T(1,128)S(1)} %bitcast.1248, f32[1,2048]{1,0:T(1,128)S(1)} %bitcast.1249, f32[1,2048]{1,0:T(1,128)S(1)} %get-tuple-element.423, f32[1,2048]{1,0:T(1,128)S(1)} %get-tuple-element.424, f32[1,2048]{1,0:T(1,128)S(1)} %get-tuple-element.425, ...), dimensions={0} | concatenate | bytes 1048576 | tf_op jit(solution)/shard_map/stack | solution.py:43
  264.1 6.0 %stack.399 = f32[64,2048]{1,0:T(8,128)} concatenate(f32[1,2048]{1,0:T(1,128)S(1)} %bitcast.1201, f32[1,2048]{1,0:T(1,128)S(1)} %bitcast.1202, f32[1,2048]{1,0:T(1,128)S(1)} %bitcast.1203, f32[1,2048]{1,0:T(1,128)S(1)} %get-tuple-element.248, f32[1,2048]{1,0:T(1,128)S(1)} %get-tuple-element.249, f32[1,2048]{1,0:T(1,128)S(1)} %get-tuple-element.250, ...), dimensions={0} | concatenate | bytes 1048576 | tf_op jit(solution)/shard_map/stack | solution.py:43
  278.0 5.8 %stack.424 = f32[64,2048]{1,0:T(8,128)} concatenate(f32[1,2048]{1,0:T(1,128)S(1)} %bitcast.1224, f32[1,2048]{1,0:T(1,128)S(1)} %bitcast.1225, f32[1,2048]{1,0:T(1,128)S(1)} %bitcast.1226, f32[1,2048]{1,0:T(1,128)S(1)} %get-tuple-element.73, f32[1,2048]{1,0:T(1,128)S(1)} %get-tuple-element.74, f32[1,2048]{1,0:T(1,128)S(1)} %get-tuple-element.75, f32[1,2048]{1,0:T(1,128)S(1)} %get-tuple-element.76, ...), dimensions={0} | concatenate | bytes 1048576 | tf_op jit(solution)/shard_map/stack | solution.py:43
  286.4 15.4 %gather_fusion.7 = f32[4096,2]{1,0:T(8,128)} fusion(f32[2,2048]{0,1:T(8,128)} %copy.309, s32[4096]{0:T(1024)S(1)} %broadcast_clamp_fusion), kind=kCustom, calls=%fused_computation.7 | custom fusion | bytes 81920 | tf_op jit(solution)/shard_map/gather | solution.py:116
  301.8 2.8 copy.310
  304.6 2.6 all-to-all-start.4
  308.6 14.2 %gather_fusion.5 = f32[4096,64]{1,0:T(8,128)} fusion(f32[64,2048]{0,1:T(8,128)S(1)} %copy.305, s32[4096]{0:T(1024)S(1)} %broadcast_clamp_fusion), kind=kCustom, calls=%fused_computation.5 | custom fusion | bytes 2113536 | tf_op jit(solution)/shard_map/gather | solution.py:115
  322.8 3.2 copy.306
  326.0 6.1 %all-to-all-start.3 = ((f32[64,32,128]{2,0,1:T(8,128)}), f32[64,32,128]{2,0,1:T(8,128)S(1)}, u32[]{:S(2)}, u32[]{:S(2)}) async-start(f32[64,32,128]{2,0,1:T(8,128)} %copy.306), calls=%async_computation.3 | async-start | bytes 2097152 | tf_op jit(solution)/shard_map/all_to_all | solution.py:118
  336.1 15.8 %gather_fusion.8 = f32[4096,2]{1,0:T(8,128)} fusion(f32[2,4096]{0,1:T(8,128)} %bitcast.540, s32[4096]{0:T(1024)S(1)} %broadcast_clamp_fusion.2), kind=kCustom, calls=%fused_computation.8 | custom fusion | bytes 81920 | tf_op jit(solution)/shard_map/gather | solution.py:124
  351.9 4.7 %select_bitcast_fusion = f32[2,4096]{0,1:T(8,128)} fusion(f32[4096,2]{1,0:T(8,128)} %gather_fusion.8, pred[4096]{0:T(1024)(128)(4,1)S(1)} %iota_compare_fusion), kind=kLoop, calls=%fused_computation.16 | loop fusion | flops 8192 | bytes 69632 | tf_op jit(solution)/shard_map/jit(_where)/select_n | solution.py:128
  356.5 2.8 copy.313
  361.3 15.8 %gather_fusion.6 = f32[4096,64]{1,0:T(8,128)} fusion(f32[64,4096]{0,1:T(8,128)} %bitcast.530, s32[4096]{0:T(1024)S(1)} %broadcast_clamp_fusion.2), kind=kCustom, calls=%fused_computation.6 | custom fusion | bytes 2113536 | tf_op jit(solution)/shard_map/gather | solution.py:123
  377.1 4.7 %bitcast_select_fusion = f32[64,4096]{0,1:T(8,128)} fusion(f32[64,4096]{0,1:T(8,128)S(1)} %copy.291, f32[4096,64]{1,0:T(8,128)} %gather_fusion.6, pred[4096]{0:T(1024)(128)(4,1)S(1)} %iota_compare_fusion), kind=kLoop, calls=%fused_computation.15 | loop fusion | flops 262144 | bytes 3149824 | tf_op jit(solution)/shard_map/jit(_where)/select_n | solution.py:127
  381.8 3.1 copy.312
  (163 shorter events, 51.8 us)
Async XLA Ops:
  0.6 6.0 %copy-start.28 = (s32[32]{0:T(128)S(1)}, s32[32]{0:T(128)}, u32[]{:S(2)}) copy-start(s32[32]{0:T(128)} %param.7) | copy-start | bytes 388
  0.6 7.9 %copy-start.26 = (s32[1,32,128]{2,1,0:T(8,128)S(1)}, s32[1,32,128]{2,1,0:T(8,128)}, u32[]{:S(2)}) copy-start(s32[1,32,128]{2,1,0:T(8,128)} %param.6) | copy-start | bytes 49156
  3.9 12.0 %collective-permute-start = (f32[5,1,16384]{2,0,1:T(8,128)S(1)}, f32[5,1,16384]{2,0,1:T(8,128)S(1)}, u32[]{:S(2)}, u32[]{:S(2)}) collective-permute-start(f32[5,1,16384]{2,0,1:T(8,128)S(1)} %copy.314), channel_id=1, source_target_pairs={{0,8},{8,16},{16,24},{24,0},{1,9},{9,17},{17,25},{25,1},{2,10},{10... | collective-permute-start | bytes 983048 | tf_op jit(solution)/shard_map/ppermute | solution.py:15
  4.6 14.0 %collective-permute-start.1 = (f32[5,1,16384]{2,0,1:T(8,128)S(1)}, f32[5,1,16384]{2,0,1:T(8,128)S(1)}, u32[]{:S(2)}, u32[]{:S(2)}) collective-permute-start(f32[5,1,16384]{2,0,1:T(8,128)S(1)} %copy.315), channel_id=1, source_target_pairs={{8,0},{16,8},{24,16},{0,24},{9,1},{17,9},{25,17},{1,25},{10,2},{18... | collective-permute-start | bytes 983048 | tf_op jit(solution)/shard_map/ppermute | solution.py:18
  88.4 48.7 %copy-start.1 = (f32[64,4096]{1,0:T(8,128)S(1)}, f32[64,4096]{1,0:T(8,128)}, u32[]{:S(2)}) copy-start(f32[64,4096]{1,0:T(8,128)} %param.5) | copy-start | bytes 3145732
  130.0 25.6 %all-to-all-start.1 = ((f32[5,32,128]{2,0,1:T(8,128)}), f32[5,32,128]{2,0,1:T(8,128)S(1)}, u32[]{:S(2)}, u32[]{:S(2)}) async-start(f32[5,32,128]{2,0,1:T(8,128)} %copy.300), calls=%async_computation.1 | async-start | bytes 262144 | tf_op jit(solution)/shard_map/all_to_all | solution.py:90
  176.2 21.6 %all-to-all-start.2 = ((f32[5,32,128]{2,0,1:T(8,128)}), f32[5,32,128]{2,0,1:T(8,128)S(1)}, u32[]{:S(2)}, u32[]{:S(2)}) async-start(f32[5,32,128]{2,0,1:T(8,128)} %copy.302), calls=%async_computation.2 | async-start | bytes 262144 | tf_op jit(solution)/shard_map/all_to_all | solution.py:104
  197.8 33.4 %all-to-all-start = ((f32[64,32,128]{2,0,1:T(8,128)}), f32[64,32,128]{2,0,1:T(8,128)S(1)}, u32[]{:S(2)}, u32[]{:S(2)}) async-start(f32[64,32,128]{2,0,1:T(8,128)} %copy.292), calls=%async_computation | async-start | bytes 2097152 | tf_op jit(solution)/shard_map/all_to_all | solution.py:103
  203.8 40.2 %copy-start.27 = (f32[63]{0:T(128)}, f32[63]{0:T(128)S(1)}, u32[]{:S(2)}) copy-start(f32[63]{0:T(128)S(1)} %multiply_multiply_fusion.2) | copy-start | bytes 760
  248.9 1.3 copy-start.3
  248.9 1.3 copy-start.4
  248.9 1.3 copy-start.5
  249.0 1.3 copy-start.6
  249.0 1.3 copy-start.7
  249.0 1.3 copy-start.8
  249.0 1.3 copy-start.9
  262.7 1.3 copy-start.12
  262.7 1.3 copy-start.13
  262.7 1.3 copy-start.14
  262.7 1.3 copy-start.15
  262.7 1.3 copy-start.16
  262.8 1.3 copy-start.17
  276.7 1.3 copy-start.20
  276.7 1.3 copy-start.21
  276.7 1.3 copy-start.22
  276.7 1.3 copy-start.23
  276.7 1.3 copy-start.24
  276.7 1.3 copy-start.25
  284.9 19.7 %copy-start = (f32[64,2048]{1,0:T(8,128)}, f32[64,2048]{1,0:T(8,128)S(1)}, u32[]{:S(2)}) copy-start(f32[64,2048]{1,0:T(8,128)S(1)} %add.9399) | copy-start | bytes 1572868
  304.6 21.3 %all-to-all-start.4 = ((f32[2,32,128]{2,0,1:T(2,128)}), f32[2,32,128]{2,0,1:T(2,128)S(1)}, u32[]{:S(2)}, u32[]{:S(2)}) async-start(f32[2,32,128]{2,0,1:T(2,128)} %copy.310), calls=%async_computation.4 | async-start | bytes 65536 | tf_op jit(solution)/shard_map/all_to_all | solution.py:119
  322.8 9.3 %copy-start.29 = (s32[32]{0:T(128)S(1)}, s32[32]{0:T(128)}, u32[]{:S(2)}) copy-start(s32[32]{0:T(128)} %param.7) | copy-start | bytes 388
  326.0 33.4 %all-to-all-start.3 = ((f32[64,32,128]{2,0,1:T(8,128)}), f32[64,32,128]{2,0,1:T(8,128)S(1)}, u32[]{:S(2)}, u32[]{:S(2)}) async-start(f32[64,32,128]{2,0,1:T(8,128)} %copy.306), calls=%async_computation.3 | async-start | bytes 2097152 | tf_op jit(solution)/shard_map/all_to_all | solution.py:118
  (5 other events, 6.4 us)
where the time goes:
time: 388 us; the launch traced here: 385 us
  local copies, waits for them, and re-layouts  272 us (70%)
  other arithmetic  61.9 us (16%)
  starting transfers between devices  29.2 us (8%)
  waiting for transfers between devices  19.9 us (5%)
    add x1, local copies, waits for them, and re-layouts, body(): 0.25 * padded[:, :-2, :] + 0.5 * padded[:, 1:-1, :]  61 us
    gather x1, local copies, waits for them, and re-layouts, body(): filtered = flat[:, cells]  40.3 us
    gather x3, other arithmetic, body(): within = column - starts[owner_of]  20.7 us
    another operation x3, local copies, waits for them, and re-layouts, thomas(): return jnp.stack(values, axis=0)  17.6 us
    gather x1, local copies, waits for them, and re-layouts, body(): send_match = match[:, send_rows].reshape(comps, devices, slots)  15.8 us
    gather x1, local copies, waits for them, and re-layouts, body(): stress = back_stress.reshape(2, devices * slots)[:, home]  15.8 us
    gather x1, local copies, waits for them, and re-layouts, body(): solved = back_prof.reshape(points, devices * slots)[:, home]  15.8 us
    gather x1, local copies, waits for them, and re-layouts, body(): ret_stress = done_stress[:, back_index].reshape(2, devices, slots)  15.4 us
  transfers between devices with their start and end apart: 7, of which 3 were waited for; matrix products, arithmetic and copies ran while one was open for 26% of the time, Pallas kernels for 0%

commit v1 on v0

v1 whole, which is shorter than its diff:
```python
import functools

import jax
import jax.numpy as jnp
from jax import lax
from jax.experimental import pallas as pl
from jax.experimental.pallas import tpu as pltpu
from jax.sharding import PartitionSpec as P

ITERS = 3
AXES = ("axial", "azim")
SUB = 8
LANE = 128


def smooth_planes(raw, filt, stride, tiles_x, sections, sems, state):
    comps = state.shape[0]
    sub = lax.broadcasted_iota(jnp.int32, (SUB, LANE), 0)
    for q in range(comps):
        pltpu.make_async_copy(state.at[q], raw.at[q], sems.at[q]).wait()

        def section(tb, carry):
            tiles = [raw[q, pl.ds((xt * sections + tb) * SUB, SUB), :] for xt in range(tiles_x)]
            ups = [pltpu.roll(tile, 1, 0) for tile in tiles]
            downs = [pltpu.roll(tile, SUB - 1, 0) for tile in tiles]
            for xt in range(tiles_x):
                below = ups[xt - 1] if xt > 0 else 0.0
                above = downs[xt + 1] if xt + 1 < tiles_x else 0.0
                low = jnp.where(sub == 0, below, ups[xt])
                high = jnp.where(sub == SUB - 1, above, downs[xt])
                at = q * stride + (xt * sections + tb) * SUB
                filt[pl.ds(pl.multiple_of(at, SUB), SUB), :] = 0.25 * (low + high) + 0.5 * tiles[xt]
            return carry

        lax.fori_loop(0, sections, section, 0, unroll=8)


def add_halo(filt, halo, start, stride, sections):
    comps = halo.shape[0]
    for q in range(comps):
        for g in range(sections // SUB):
            rows = pl.ds(q * stride + start + g * SUB * SUB, SUB, stride=SUB)
            filt[rows, :] = filt[rows, :] + 0.25 * halo[q, pl.ds(g * SUB, SUB), :]


def gather_kernel(tiles_x, sections, stride, rows, lanes, state, low, high, out, raw, filt, sems):
    comps = state.shape[0]
    groups = out.shape[0]
    for q in range(comps):
        pltpu.make_async_copy(state.at[q], raw.at[q], sems.at[q]).start()
    smooth_planes(raw, filt, stride, tiles_x, sections, sems, state)
    add_halo(filt, low, 0, stride, sections)
    add_halo(filt, high, (tiles_x - 1) * sections * SUB + SUB - 1, stride, sections)
    lane = lax.broadcasted_iota(jnp.int32, (SUB, LANE), 1)

    def group(e, carry):
        wanted = jnp.broadcast_to(lanes[pl.ds(e, 1), :], (SUB, LANE))
        found = jnp.zeros((SUB, LANE), jnp.float32)
        for k in range(LANE):
            cell = filt[pl.ds(rows[e, k], SUB, stride=stride), :]
            cell = jnp.take_along_axis(cell, wanted, axis=1)
            found = jnp.where(lane == k, cell, found)
        out[e] = found
        return carry

    lax.fori_loop(0, groups, group, 0)


def solve_kernel(points, width, live, profile, match, new_profile, wall_stress):
    step = 1.0 / (points - 1)
    inv_step = float(points - 1)
    tiles = points // SUB
    sub = lax.broadcasted_iota(jnp.int32, (SUB, LANE), 0)
    lane = lax.broadcasted_iota(jnp.int32, (1, LANE), 1)
    index = [(sub + t * SUB).astype(jnp.float32) for t in range(tiles)]
    mixing = [0.41 * (i + 0.5) * step for i in index]
    mix_sq = [m * m for m in mixing]
    first = pl.program_id(0) * width

    def spread(row):
        return jnp.broadcast_to(row, (SUB, LANE))

    for cb in range(width // LANE):
        cols = pl.ds(cb * LANE, LANE)
        m = [spread(match[cb, q : q + 1, :]) for q in range(5)]
        visc = 0.01 * jnp.exp(0.5 * m[4])
        sigma = (0.5 * step) * m[3]
        speed = jnp.sqrt(m[1] * m[1] + m[2] * m[2] + 0.25)
        old = [profile[pl.ds(t * SUB, SUB), cols] for t in range(tiles)]
        turned = [pltpu.roll(u, SUB - 1, 0) for u in old]
        grad = []
        for t in range(tiles):
            after = turned[t + 1] if t + 1 < tiles else old[t]
            grad.append((jnp.where(sub == SUB - 1, after, turned[t]) - old[t]) * inv_step)
        for sweep in range(ITERS):
            weight_sum = jnp.zeros((SUB, LANE), jnp.float32)
            known_sum = jnp.zeros((SUB, LANE), jnp.float32)
            weights = []
            knowns = []
            for t in range(tiles):
                square = grad[t] * grad[t]
                over = square + 1.0
                inv_root = lax.rsqrt(over)
                viscous = visc + mix_sq[t] * (over * inv_root)
                excess = mix_sq[t] * (square * inv_root)
                weight = 1.0 / (viscous + excess)
                if t == tiles - 1:
                    weight = jnp.where(sub == SUB - 1, 0.0, weight)
                known = (excess * grad[t] + sigma * index[t]) * weight
                weight_sum = weight_sum + weight
                known_sum = known_sum + known
                weights.append(weight)
                knowns.append(known)
            weight_all = spread(jnp.sum(weight_sum, axis=0, keepdims=True))
            known_all = spread(jnp.sum(known_sum, axis=0, keepdims=True))
            flux = (inv_step * speed - known_all) / weight_all
            grad = [knowns[t] + flux * weights[t] for t in range(tiles)]
        burning = lane + (first + cb * LANE) < live[0]
        burn = spread(burning.astype(jnp.int32)) > 0
        carry = jnp.zeros((SUB, LANE), jnp.float32)
        for t in range(tiles):
            total = grad[t]
            for hop in (1, 2, 4):
                total = total + jnp.where(sub >= hop, pltpu.roll(total, hop, 0), 0.0)
            before = jnp.where(sub >= 1, pltpu.roll(total, 1, 0), 0.0)
            new_profile[pl.ds(t * SUB, SUB), cols] = jnp.where(
                burn, (before + carry) * step, old[t]
            )
            carry = carry + spread(total[SUB - 1 : SUB, :])
        shear = jnp.exp(0.3 * m[0]) * visc * spread(grad[0][0:1, :])
        for row, part in enumerate((m[1], m[2])):
            wall_stress[row : row + 1, cols] = jnp.where(burn, shear * part / speed, 0.0)[0:1, :]


def solve(profile, match, live):
    points, owned = profile.shape
    width = min(1024, owned)
    return pl.pallas_call(
        functools.partial(solve_kernel, points, width),
        grid=(owned // width,),
        out_shape=(
            jax.ShapeDtypeStruct((points, owned), jnp.float32),
            jax.ShapeDtypeStruct((2, owned), jnp.float32),
        ),
        in_specs=[
            pl.BlockSpec(memory_space=pltpu.SMEM),
            pl.BlockSpec((points, width), lambda i: (0, i)),
            pl.BlockSpec((width // LANE, SUB, LANE), lambda i: (i, 0, 0)),
        ],
        out_specs=(
            pl.BlockSpec((points, width), lambda i: (0, i)),
            pl.BlockSpec((2, width), lambda i: (0, i)),
        ),
        compiler_params=pltpu.CompilerParams(vmem_limit_bytes=32 << 20),
        name="wall_solve",
    )(live, profile, match)


def body(state, profile, samp_cell, own_live):
    comps, slab, section = state.shape
    owned = profile.shape[1]
    devices = lax.axis_size(AXES)
    slots = samp_cell.shape[2]
    here = lax.axis_index(AXES)
    groups = owned // LANE
    tiles_x = slab // SUB
    sections = section // LANE
    plane = slab * sections
    stride = plane + SUB
    cells = samp_cell.reshape(groups, LANE)
    at_x = cells // section
    at_t = cells % section
    rows = ((at_x // SUB) * sections + at_t // LANE) * SUB + at_x % SUB
    lanes = at_t % LANE
    count = lax.axis_size("axial")
    forward = [(i, (i + 1) % count) for i in range(count)]
    backward = [((i + 1) % count, i) for i in range(count)]
    low = lax.ppermute(state[:, slab - 1, :], "axial", forward).reshape(comps, sections, LANE)
    high = lax.ppermute(state[:, 0, :], "axial", backward).reshape(comps, sections, LANE)
    view = state.reshape(comps, tiles_x, SUB, sections, LANE)
    view = view.transpose(0, 1, 3, 2, 4).reshape(comps, plane, LANE)
    sampled = pl.pallas_call(
        functools.partial(gather_kernel, tiles_x, sections, stride),
        out_shape=jax.ShapeDtypeStruct((groups, SUB, LANE), jnp.float32),
        in_specs=[
            pl.BlockSpec(memory_space=pltpu.SMEM),
            pl.BlockSpec(memory_space=pltpu.VMEM),
            pl.BlockSpec(memory_space=pl.ANY),
            pl.BlockSpec(memory_space=pltpu.VMEM),
            pl.BlockSpec(memory_space=pltpu.VMEM),
        ],
        out_specs=pl.BlockSpec(memory_space=pltpu.VMEM),
        scratch_shapes=[
            pltpu.VMEM((comps, plane, LANE), jnp.float32),
            pltpu.VMEM((SUB * stride, LANE), jnp.float32),
            pltpu.SemaphoreType.DMA((comps,)),
        ],
        compiler_params=pltpu.CompilerParams(vmem_limit_bytes=40 << 20),
        name="sample_cells",
    )(rows, lanes, view, low, high)
    if slots == LANE:
        match = lax.all_to_all(sampled, AXES, split_axis=0, concat_axis=0, tiled=True)
    else:
        outgoing = sampled.transpose(1, 0, 2).reshape(SUB, devices, slots)
        arrived = lax.all_to_all(outgoing, AXES, split_axis=1, concat_axis=1, tiled=True)
        match = arrived.reshape(SUB, groups, LANE).transpose(1, 0, 2)
    live = lax.dynamic_slice(own_live, (here,), (1,))
    return solve(profile, match, live)


def solution(mesh):
    return jax.shard_map(
        body,
        mesh=mesh,
        in_specs=(
            P(None, "axial", "azim"),
            P(None, AXES),
            P(AXES, None, None),
            P(),
        ),
        out_specs=(P(None, AXES), P(None, AXES)),
        check_vma=False,
    )
```

time: 388 us -> 51.3 us (0.13)
  local copies, waits for them, and re-layouts: 272 us -> 6.76 us
  other arithmetic: 61.9 us -> 0.77 us
  starting transfers between devices: 29.2 us -> 8.31 us
  Pallas kernels: 0 us -> 15.2 us
    gather x13 -> x0, local copies, waits for them, and re-layouts: 154 us -> none  [the longest x1 40.3 us: body(): filtered = flat[:, cells]]
    add x2 -> x0, local copies, waits for them, and re-layouts: 62.4 us -> none  [the longest x1 61 us: body(): 0.25 * padded[:, :-2, :] + 0.5 * padded[:, 1:-1, :]]
    all_to_all x5 -> x1, starting transfers between devices: 26.6 us -> 5.8 us  [body(): lax.all_to_all(sampled, AXES, split_axis=0, concat_axis=0, tiled=True)]
    gather x8 -> x0, other arithmetic: 20.7 us -> none  [the longest x3 20.7 us: body(): within = column - starts[owner_of]]
    another operation x5 -> x0, local copies, waits for them, and re-layouts: 19 us -> none  [the longest x3 17.6 us: thomas(): return jnp.stack(values, axis=0)]
    pallas_call x0 -> x2, Pallas kernels: none -> 15.2 us  [the longest x1 10.5 us: body(): pl.pallas_call(functools.partial(gather_kernel, tiles_x, sections, stride...]
    reshape x5 -> x0, local copies, waits for them, and re-layouts: 13.3 us -> none  [the longest x1 3.16 us: body(): ret_prof = done_prof[:, back_index].reshape(points, devices, slots)]
    add x6 -> x0, other arithmetic: 11.8 us -> none  [the longest x1 8.41 us: body(): 0.25 * padded[:, :-2, :] + 0.5 * padded[:, 1:-1, :]]
  transfers between devices with their start and end apart: 7 -> 3, of which waited for: 3 -> 3; matrix products, arithmetic and copies ran while one was open for 26% -> 3% of each run, Pallas kernels for 0% -> 0%
where the time goes in v1:
time: 51.3 us; the launch traced here: 51.1 us
  waiting for transfers between devices  19.3 us (38%)
  Pallas kernels  15.2 us (30%)
  starting transfers between devices  8.31 us (16%)
  local copies, waits for them, and re-layouts  6.76 us (13%)
  other arithmetic  0.77 us (2%)
  between operations  0.72 us (1%)
    ppermute x1, waiting for transfers between devices, body(): lax.ppermute(state[:, 0, :], 'axial', backward)  11 us
    pallas_call x1, Pallas kernels, body(): pl.pallas_call(functools.partial(gather_kernel, tiles_x, sections, stride...  10.5 us
    all_to_all x1, waiting for transfers between devices, body(): lax.all_to_all(sampled, AXES, split_axis=0, concat_axis=0, tiled=True)  7.07 us
    all_to_all x1, starting transfers between devices, body(): lax.all_to_all(sampled, AXES, split_axis=0, concat_axis=0, tiled=True)  5.8 us
    pallas_call x1, Pallas kernels, solve(): pl.pallas_call(functools.partial(solve_kernel, points, width), grid=(owne...  4.75 us
    slice x1, local copies, waits for them, and re-layouts, body(): state[:, 0, :]  3.07 us
    unnamed x10, local copies, waits for them, and re-layouts  3.03 us
    ppermute x1, starting transfers between devices, body(): lax.ppermute(state[:, 0, :], 'axial', backward)  2.46 us
  transfers between devices with their start and end apart: 3, of which 3 were waited for; matrix products, arithmetic and copies ran while one was open for 3% of the time, Pallas kernels for 0%

profile of v1, /device:TPU:0, one launch (start us, length us, event | category | flops | bytes accessed | tf_op | source)
XLA Modules:
  0.0 51.1 jit_solution(14657592272255073316)
XLA Ops:
  0.6 0.0 copy-start.2
  0.6 0.0 copy-start.1
  0.6 3.1 %fusion.11 = (f32[5,1,16384]{2,1,0:T(1,128)S(1)}, f32[5,1,16384]{2,1,0:T(1,128)S(1)}) fusion(f32[5,16,16384]{2,1,0:T(8,128)} %param.4), kind=kLoop, calls=%fused_computation.35 | loop fusion | bytes 1310720 | tf_op jit(solution)/shard_map/slice | solution.py:179
  3.7 0.2 copy.16
  3.9 2.5 %collective-permute-start.1 = (f32[5,16384]{1,0:T(8,128)S(1)}, f32[5,16384]{1,0:T(8,128)S(1)}, u32[]{:S(2)}, u32[]{:S(2)}) collective-permute-start(f32[5,16384]{1,0:T(8,128)S(1)} %bitcast.48), channel_id=1, source_target_pairs={{8,0},{16,8},{24,16},{0,24},{9,1},{17,9},{25,17},{1,25},{10,2},{18... | collective-permute-start | bytes 983048 | tf_op jit(solution)/shard_map/ppermute | solution.py:179
  6.4 0.2 copy.17
  6.6 0.1 collective-permute-start
  6.7 0.8 %add_select_fusion = (s32[32,128]{1,0:T(8,128)S(1)}, s32[32,128]{1,0:T(8,128)S(1)}) fusion(s32[1,32,128]{2,1,0:T(8,128)} %param.6), kind=kLoop, calls=%fused_computation.4 | loop fusion | flops 249856 | bytes 49152 | tf_op jit(solution)/shard_map/jit(remainder)/select_n | solution.py:174
  7.4 11.0 %collective-permute-done.1 = f32[5,16384]{1,0:T(8,128)S(1)} collective-permute-done((f32[5,16384]{1,0:T(8,128)S(1)}, f32[5,16384]{1,0:T(8,128)S(1)}, u32[]{:S(2)}, u32[]{:S(2)}) %collective-permute-start.1) | collective-permute-done | bytes 327712 | tf_op jit(solution)/shard_map/ppermute | solution.py:179
  18.4 0.1 copy.18
  18.5 1.2 %collective-permute-done = f32[5,16384]{1,0:T(8,128)S(1)} collective-permute-done((f32[5,16384]{1,0:T(8,128)S(1)}, f32[5,16384]{1,0:T(8,128)S(1)}, u32[]{:S(2)}, u32[]{:S(2)}) %collective-permute-start) | collective-permute-done | bytes 327712 | tf_op jit(solution)/shard_map/ppermute | solution.py:178
  19.7 0.1 copy.19
  19.8 0.0 copy-start
  19.8 2.5 %copy-done = f32[5,16,16384]{2,1,0:T(8,128)S(1)} copy-done((f32[5,16,16384]{2,1,0:T(8,128)S(1)}, f32[5,16,16384]{2,1,0:T(8,128)}, u32[]{:S(2)}) %copy-start) | copy-done | bytes 5242904
  22.3 10.5 %sample_cells.1 = f32[32,8,128]{2,1,0:T(8,128)} custom-call(s32[32,128]{1,0:T(8,128)S(1)} %get-tuple-element.5.rows, s32[32,128]{1,0:T(8,128)S(1)} %get-tuple-element.4.lanes, f32[5,2048,128]{2,1,0:T(8,128)S(1)} %bitcast.45, f32[5,128,128]{2,1,0:T(8,128)S(1)} %bitcast.47, f32[5,128,128]{2,1,0:T(8,128)S(1)} %bitcast.46), custom_call_target="tpu_custom_call" | custom-call | tf_op jit(solution)/shard_map/sample_cells/pallas_call | solution.py:182
  32.8 5.8 %all-to-all-start = ((f32[32,8,128]{2,1,0:T(8,128)}), f32[32,8,128]{2,1,0:T(8,128)S(1)}, u32[]{:S(2)}, u32[]{:S(2)}) async-start(f32[32,8,128]{2,1,0:T(8,128)} %sample_cells.1), calls=%async_computation | async-start | bytes 262144 | tf_op jit(solution)/shard_map/all_to_all | solution.py:202
  38.6 0.0 copy-done.2
  38.6 0.7 %dynamic_slice.3.live = s32[1]{0:T(128)} dynamic-slice(s32[32]{0:T(128)S(1)} %copy-done.2, s32[]{:T(128)S(6)} %select_n.29), dynamic_slice_sizes={1} | dynamic-slice | bytes 12 | tf_op jit(solution)/shard_map/dynamic_slice | solution.py:207
  39.3 7.1 %all-to-all-done.match = f32[32,8,128]{2,1,0:T(8,128)S(1)} async-done(((f32[32,8,128]{2,1,0:T(8,128)}), f32[32,8,128]{2,1,0:T(8,128)S(1)}, u32[]{:S(2)}, u32[]{:S(2)}) %all-to-all-start) | async-done | bytes 131104 | tf_op jit(solution)/shard_map/all_to_all | solution.py:202
  46.3 0.0 copy-done.1
  46.3 4.7 %wall_solve.1 = (f32[64,4096]{1,0:T(8,128)}, f32[2,4096]{1,0:T(2,128)}) custom-call(s32[1]{0:T(128)} %dynamic_slice.3.live, f32[64,4096]{1,0:T(8,128)S(1)} %copy-done.1, f32[32,8,128]{2,1,0:T(8,128)S(1)} %all-to-all-done.match), custom_call_target="tpu_custom_call" | custom-call | tf_op jit(solution)/shard_map/wall_solve/pallas_call | solution.py:138
Async XLA Ops:
  0.6 38.0 %copy-start.2 = (s32[32]{0:T(128)S(1)}, s32[32]{0:T(128)}, u32[]{:S(2)}) copy-start(s32[32]{0:T(128)} %param.7) | copy-start | bytes 388
  0.6 45.7 %copy-start.1 = (f32[64,4096]{1,0:T(8,128)S(1)}, f32[64,4096]{1,0:T(8,128)}, u32[]{:S(2)}) copy-start(f32[64,4096]{1,0:T(8,128)} %profile.1) | copy-start | bytes 3145732
  3.9 14.5 %collective-permute-start.1 = (f32[5,16384]{1,0:T(8,128)S(1)}, f32[5,16384]{1,0:T(8,128)S(1)}, u32[]{:S(2)}, u32[]{:S(2)}) collective-permute-start(f32[5,16384]{1,0:T(8,128)S(1)} %bitcast.48), channel_id=1, source_target_pairs={{8,0},{16,8},{24,16},{0,24},{9,1},{17,9},{25,17},{1,25},{10,2},{18... | collective-permute-start | bytes 983048 | tf_op jit(solution)/shard_map/ppermute | solution.py:179
  6.6 13.1 %collective-permute-start = (f32[5,16384]{1,0:T(8,128)S(1)}, f32[5,16384]{1,0:T(8,128)S(1)}, u32[]{:S(2)}, u32[]{:S(2)}) collective-permute-start(f32[5,16384]{1,0:T(8,128)S(1)} %bitcast.50), channel_id=1, source_target_pairs={{0,8},{8,16},{16,24},{24,0},{1,9},{9,17},{17,25},{25,1},{2,10},{10... | collective-permute-start | bytes 983048 | tf_op jit(solution)/shard_map/ppermute | solution.py:178
  19.8 2.5 %copy-start = (f32[5,16,16384]{2,1,0:T(8,128)S(1)}, f32[5,16,16384]{2,1,0:T(8,128)}, u32[]{:S(2)}) copy-start(f32[5,16,16384]{2,1,0:T(8,128)} %param.4) | copy-start | bytes 15728644
  32.8 13.5 %all-to-all-start = ((f32[32,8,128]{2,1,0:T(8,128)}), f32[32,8,128]{2,1,0:T(8,128)S(1)}, u32[]{:S(2)}, u32[]{:S(2)}) async-start(f32[32,8,128]{2,1,0:T(8,128)} %sample_cells.1), calls=%async_computation | async-start | bytes 262144 | tf_op jit(solution)/shard_map/all_to_all | solution.py:202

commit v2 on v1

--- a/solution.py
+++ b/solution.py
@@ -20,7 +20,7 @@
         pltpu.make_async_copy(state.at[q], raw.at[q], sems.at[q]).wait()
 
         def section(tb, carry):
-            tiles = [raw[q, pl.ds((xt * sections + tb) * SUB, SUB), :] for xt in range(tiles_x)]
+            tiles = [raw[q, xt, tb] for xt in range(tiles_x)]
             ups = [pltpu.roll(tile, 1, 0) for tile in tiles]
             downs = [pltpu.roll(tile, SUB - 1, 0) for tile in tiles]
             for xt in range(tiles_x):
@@ -35,35 +35,131 @@
         lax.fori_loop(0, sections, section, 0, unroll=8)
 
 
-def add_halo(filt, halo, start, stride, sections):
-    comps = halo.shape[0]
-    for q in range(comps):
-        for g in range(sections // SUB):
-            rows = pl.ds(q * stride + start + g * SUB * SUB, SUB, stride=SUB)
-            filt[rows, :] = filt[rows, :] + 0.25 * halo[q, pl.ds(g * SUB, SUB), :]
-
-
-def gather_kernel(tiles_x, sections, stride, rows, lanes, state, low, high, out, raw, filt, sems):
+def add_halo(filt, halo, start, sections):
+    for g in range(sections // SUB):
+        rows = pl.ds(start + g * SUB * SUB, SUB, stride=SUB)
+        filt[rows, :] = filt[rows, :] + 0.25 * halo[pl.ds(g * SUB, SUB), :]
+
+
+def sample_kernel(
+    names,
+    sizes,
+    cells,
+    state,
+    out,
+    raw,
+    filt,
+    halo,
+    stage,
+    rows_v,
+    rows,
+    sems,
+    halo_send,
+    halo_recv,
+    row_sem,
+    send_sem,
+    recv_sem,
+):
+    tiles_x, sections, stride = sizes
     comps = state.shape[0]
-    groups = out.shape[0]
+    groups = stage.shape[0]
+    devices = out.shape[0]
+    share = devices // groups
+    axial, azim = names
+    a, z = lax.axis_index(axial), lax.axis_index(azim)
+    count, width = lax.axis_size(axial), lax.axis_size(azim)
+    me = a * width + z
+
+    def place(d):
+        return (d // width, d % width)
+
     for q in range(comps):
         pltpu.make_async_copy(state.at[q], raw.at[q], sems.at[q]).start()
+
+    barrier = pltpu.get_barrier_semaphore()
+
+    def greet(j, carry):
+        pl.semaphore_signal(
+            barrier, inc=1, device_id=place((me + j) % devices), device_id_type=pl.DeviceIdType.MESH
+        )
+        return carry
+
+    lax.fori_loop(1, devices, greet, 0)
+
+    cell = cells[...]
+    section = sections * LANE
+    at_x = cell // section
+    at_t = cell % section
+    rows_v[...] = ((at_x // SUB) * sections + at_t // LANE) * SUB + at_x % SUB
+    row_copy = pltpu.make_async_copy(rows_v, rows, row_sem)
+    row_copy.start()
+    pl.semaphore_wait(barrier, devices - 1)
+
+    halos = []
+    for q in range(comps):
+        for side in range(2):
+            if side == 0:
+                edge = state.at[q, tiles_x - 1, :, SUB - 1, :]
+                target = (a + 1) % count
+            else:
+                edge = state.at[q, 0, :, 0, :]
+                target = (a + count - 1) % count
+            copy = pltpu.make_async_remote_copy(
+                src_ref=edge,
+                dst_ref=halo.at[side, q],
+                send_sem=halo_send.at[side, q],
+                recv_sem=halo_recv.at[side, q],
+                device_id=(target, z),
+                device_id_type=pl.DeviceIdType.MESH,
+            )
+            copy.start()
+            halos.append(copy)
+
+    filt[pl.ds(comps * stride, (SUB - comps) * stride), :] = jnp.zeros(
+        ((SUB - comps) * stride, LANE), jnp.float32
+    )
     smooth_planes(raw, filt, stride, tiles_x, sections, sems, state)
-    add_halo(filt, low, 0, stride, sections)
-    add_halo(filt, high, (tiles_x - 1) * sections * SUB + SUB - 1, stride, sections)
+    last = (tiles_x - 1) * sections * SUB + SUB - 1
+    for q in range(comps):
+        for side in range(2):
+            halos[2 * q + side].wait()
+            add_halo(filt, halo.at[side, q], q * stride + (0 if side == 0 else last), sections)
+    row_copy.wait()
     lane = lax.broadcasted_iota(jnp.int32, (SUB, LANE), 1)
 
-    def group(e, carry):
-        wanted = jnp.broadcast_to(lanes[pl.ds(e, 1), :], (SUB, LANE))
+    def group(j, carry):
+        g = (me // share + 1 + j) % groups
+        wanted = jnp.broadcast_to(cells[pl.ds(g, 1), :] % LANE, (SUB, LANE))
         found = jnp.zeros((SUB, LANE), jnp.float32)
         for k in range(LANE):
-            cell = filt[pl.ds(rows[e, k], SUB, stride=stride), :]
-            cell = jnp.take_along_axis(cell, wanted, axis=1)
-            found = jnp.where(lane == k, cell, found)
-        out[e] = found
+            piece = filt[pl.ds(rows[g, k], SUB, stride=stride), :]
+            piece = jnp.take_along_axis(piece, wanted, axis=1)
+            found = jnp.where(lane == k, piece, found)
+        stage[g] = found
+        for r in range(share):
+            owner = g * share + r
+
+            @pl.when(owner != me)
+            def _():
+                pltpu.make_async_remote_copy(
+                    src_ref=stage.at[g],
+                    dst_ref=out.at[me],
+                    send_sem=send_sem,
+                    recv_sem=recv_sem,
+                    device_id=place(owner),
+                    device_id_type=pl.DeviceIdType.MESH,
+                ).start()
+
+            @pl.when(owner == me)
+            def _():
+                out[me] = found
+
         return carry
 
     lax.fori_loop(0, groups, group, 0)
+    every = out.at[pl.ds(0, devices - 1)]
+    pltpu.make_async_copy(every, every, recv_sem).wait()
+    pltpu.make_async_copy(every, every, send_sem).wait()
 
 
 def solve_kernel(points, width, live, profile, match, new_profile, wall_stress):
@@ -168,42 +264,39 @@
     plane = slab * sections
     stride = plane + SUB
     cells = samp_cell.reshape(groups, LANE)
-    at_x = cells // section
-    at_t = cells % section
-    rows = ((at_x // SUB) * sections + at_t // LANE) * SUB + at_x % SUB
-    lanes = at_t % LANE
-    count = lax.axis_size("axial")
-    forward = [(i, (i + 1) % count) for i in range(count)]
-    backward = [((i + 1) % count, i) for i in range(count)]
-    low = lax.ppermute(state[:, slab - 1, :], "axial", forward).reshape(comps, sections, LANE)
-    high = lax.ppermute(state[:, 0, :], "axial", backward).reshape(comps, sections, LANE)
-    view = state.reshape(comps, tiles_x, SUB, sections, LANE)
-    view = view.transpose(0, 1, 3, 2, 4).reshape(comps, plane, LANE)
-    sampled = pl.pallas_call(
-        functools.partial(gather_kernel, tiles_x, sections, stride),
-        out_shape=jax.ShapeDtypeStruct((groups, SUB, LANE), jnp.float32),
+    view = state.reshape(comps, tiles_x, SUB, sections, LANE).transpose(0, 1, 3, 2, 4)
+    arrived = pl.pallas_call(
+        functools.partial(sample_kernel, AXES, (tiles_x, sections, stride)),
+        out_shape=jax.ShapeDtypeStruct((devices, SUB, LANE), jnp.float32),
         in_specs=[
-            pl.BlockSpec(memory_space=pltpu.SMEM),
             pl.BlockSpec(memory_space=pltpu.VMEM),
             pl.BlockSpec(memory_space=pl.ANY),
-            pl.BlockSpec(memory_space=pltpu.VMEM),
-            pl.BlockSpec(memory_space=pltpu.VMEM),
         ],
         out_specs=pl.BlockSpec(memory_space=pltpu.VMEM),
         scratch_shapes=[
-            pltpu.VMEM((comps, plane, LANE), jnp.float32),
+            pltpu.VMEM((comps, tiles_x, sections, SUB, LANE), jnp.float32),
             pltpu.VMEM((SUB * stride, LANE), jnp.float32),
+            pltpu.VMEM((2, comps, sections, LANE), jnp.float32),
+            pltpu.VMEM((groups, SUB, LANE), jnp.float32),
+            pltpu.VMEM((groups, LANE), jnp.int32),
+            pltpu.SMEM((groups, LANE), jnp.int32),
             pltpu.SemaphoreType.DMA((comps,)),
+            pltpu.SemaphoreType.DMA((2, comps)),
+            pltpu.SemaphoreType.DMA((2, comps)),
+            pltpu.SemaphoreType.DMA,
+            pltpu.SemaphoreType.DMA,
+            pltpu.SemaphoreType.DMA,
         ],
-        compiler_params=pltpu.CompilerParams(vmem_limit_bytes=40 << 20),
+        compiler_params=pltpu.CompilerParams(
+            vmem_limit_bytes=60 << 20, collective_id=0, has_side_effects=True
+        ),
         name="sample_cells",
-    )(rows, lanes, view, low, high)
+    )(cells, view)
     if slots == LANE:
-        match = lax.all_to_all(sampled, AXES, split_axis=0, concat_axis=0, tiled=True)
+        match = arrived
     else:
-        outgoing = sampled.transpose(1, 0, 2).reshape(SUB, devices, slots)
-        arrived = lax.all_to_all(outgoing, AXES, split_axis=1, concat_axis=1, tiled=True)
-        match = arrived.reshape(SUB, groups, LANE).transpose(1, 0, 2)
+        own = lax.dynamic_slice_in_dim(arrived, here % (LANE // slots) * slots, slots, axis=2)
+        match = own.transpose(1, 0, 2).reshape(SUB, groups, LANE).transpose(1, 0, 2)
     live = lax.dynamic_slice(own_live, (here,), (1,))
     return solve(profile, match, live)
 

time: 51.3 us -> 33.6 us (0.65)
  waiting for transfers between devices: 19.3 us -> 0 us
  Pallas kernels: 15.2 us -> 30.3 us
  starting transfers between devices: 8.31 us -> 0 us
  local copies, waits for them, and re-layouts: 6.76 us -> 2.28 us
  other arithmetic: 0.77 us -> 0 us
    pallas_call x1, Pallas kernels: 10.5 us -> 25.6 us  [body(): pl.pallas_call(functools.partial(sample_kernel, AXES, (tiles_x, sections,...]
    ppermute x2 -> x0, waiting for transfers between devices: 12.2 us -> none  [the longest x1 11 us: body(): lax.ppermute(state[:, 0, :], 'axial', backward)]
    all_to_all x1 -> x0, waiting for transfers between devices: 7.07 us -> none  [body(): lax.all_to_all(sampled, AXES, split_axis=0, concat_axis=0, tiled=True)]
    all_to_all x1 -> x0, starting transfers between devices: 5.8 us -> none  [body(): lax.all_to_all(sampled, AXES, split_axis=0, concat_axis=0, tiled=True)]
    slice x1 -> x0, local copies, waits for them, and re-layouts: 3.07 us -> none  [body(): state[:, 0, :]]
    ppermute x2 -> x0, starting transfers between devices: 2.52 us -> none  [the longest x1 2.46 us: body(): lax.ppermute(state[:, 0, :], 'axial', backward)]
    unnamed x10 -> x4, local copies, waits for them, and re-layouts: 3.03 us -> 0.9 us
    select_n x1 -> x0, other arithmetic: 0.77 us -> none  [body(): lanes = at_t % LANE]
  transfers between devices with their start and end apart: 3 -> 0, of which waited for: 3 -> 0; matrix products, arithmetic and copies ran while one was open for 3% -> 0% of each run, Pallas kernels for 0% -> 0%
where the time goes in v2:
time: 33.6 us; the launch traced here: 33.3 us
  Pallas kernels  30.3 us (90%)
  local copies, waits for them, and re-layouts  2.28 us (7%)
  between operations  0.67 us (2%)
    pallas_call x1, Pallas kernels, body(): pl.pallas_call(functools.partial(sample_kernel, AXES, (tiles_x, sections,...  25.6 us
    pallas_call x1, Pallas kernels, solve(): pl.pallas_call(functools.partial(solve_kernel, points, width), grid=(owne...  4.69 us
    dynamic_slice x1, local copies, waits for them, and re-layouts, body(): live = lax.dynamic_slice(own_live, (here,), (1,))  1.38 us
    unnamed x4, local copies, waits for them, and re-layouts  0.9 us

profile of v2, /device:TPU:0, one launch (start us, length us, event | category | flops | bytes accessed | tf_op | source)
XLA Modules:
  0.0 33.3 jit_solution(10367264137870965697)
XLA Ops:
  0.6 0.0 copy-start
  0.6 1.4 %dynamic_slice.3.live = s32[1]{0:T(128)} dynamic-slice(s32[32]{0:T(128)} %param.7, s32[]{:T(128)S(6)} %select_n.3), dynamic_slice_sizes={1} | dynamic-slice | bytes 12 | tf_op jit(solution)/shard_map/dynamic_slice | solution.py:300
  2.0 25.6 %sample_cells.1.match = f32[32,8,128]{2,1,0:T(8,128)} custom-call(s32[32,128]{1,0:T(8,128)} %bitcast.5, f32[5,2,128,8,128]{4,3,2,1,0:T(8,128)} %bitcast.4), custom_call_target="tpu_custom_call" | custom-call | tf_op jit(solution)/shard_map/sample_cells/pallas_call | solution.py:268
  27.7 0.0 copy-done
  27.7 0.0 copy-start.1
  27.7 0.9 %copy-done.1 = f32[32,8,128]{2,1,0:T(8,128)S(1)} copy-done((f32[32,8,128]{2,1,0:T(8,128)S(1)}, f32[32,8,128]{2,1,0:T(8,128)}, u32[]{:S(2)}) %copy-start.1) | copy-done | bytes 131096
  28.6 4.7 %wall_solve.1 = (f32[64,4096]{1,0:T(8,128)}, f32[2,4096]{1,0:T(2,128)}) custom-call(s32[1]{0:T(128)} %dynamic_slice.3.live, f32[64,4096]{1,0:T(8,128)S(1)} %copy-done, f32[32,8,128]{2,1,0:T(8,128)S(1)} %copy-done.1), custom_call_target="tpu_custom_call" | custom-call | tf_op jit(solution)/shard_map/wall_solve/pallas_call | solution.py:234
Async XLA Ops:
  0.6 27.1 %copy-start = (f32[64,4096]{1,0:T(8,128)S(1)}, f32[64,4096]{1,0:T(8,128)}, u32[]{:S(2)}) copy-start(f32[64,4096]{1,0:T(8,128)} %profile.1) | copy-start | bytes 3145732
  27.7 0.9 %copy-start.1 = (f32[32,8,128]{2,1,0:T(8,128)S(1)}, f32[32,8,128]{2,1,0:T(8,128)}, u32[]{:S(2)}) copy-start(f32[32,8,128]{2,1,0:T(8,128)} %sample_cells.1.match) | copy-start | bytes 393220

commit v3 on v2

--- a/solution.py
+++ b/solution.py
@@ -11,6 +11,8 @@
 AXES = ("axial", "azim")
 SUB = 8
 LANE = 128
+WIDE = 256
+PARTS = 4
 
 
 def smooth_planes(raw, filt, stride, tiles_x, sections, sems, state):
@@ -130,11 +132,14 @@
     def group(j, carry):
         g = (me // share + 1 + j) % groups
         wanted = jnp.broadcast_to(cells[pl.ds(g, 1), :] % LANE, (SUB, LANE))
-        found = jnp.zeros((SUB, LANE), jnp.float32)
+        parts = [jnp.zeros((SUB, LANE), jnp.float32)] * PARTS
         for k in range(LANE):
             piece = filt[pl.ds(rows[g, k], SUB, stride=stride), :]
             piece = jnp.take_along_axis(piece, wanted, axis=1)
-            found = jnp.where(lane == k, piece, found)
+            parts[k % PARTS] = jnp.where(lane == k, piece, parts[k % PARTS])
+        found = parts[0]
+        for i in range(1, PARTS):
+            found = jnp.where(lane % PARTS == i, parts[i], found)
         stage[g] = found
         for r in range(share):
             owner = g * share + r
@@ -162,23 +167,27 @@
     pltpu.make_async_copy(every, every, send_sem).wait()
 
 
-def solve_kernel(points, width, live, profile, match, new_profile, wall_stress):
+def solve_kernel(names, points, width, live, profile, match, new_profile, wall_stress):
     step = 1.0 / (points - 1)
     inv_step = float(points - 1)
     tiles = points // SUB
-    sub = lax.broadcasted_iota(jnp.int32, (SUB, LANE), 0)
-    lane = lax.broadcasted_iota(jnp.int32, (1, LANE), 1)
+    sub = lax.broadcasted_iota(jnp.int32, (SUB, WIDE), 0)
+    lane = lax.broadcasted_iota(jnp.int32, (1, WIDE), 1)
     index = [(sub + t * SUB).astype(jnp.float32) for t in range(tiles)]
     mixing = [0.41 * (i + 0.5) * step for i in index]
     mix_sq = [m * m for m in mixing]
     first = pl.program_id(0) * width
+    live_here = live[lax.axis_index(names[0]) * lax.axis_size(names[1]) + lax.axis_index(names[1])]
 
     def spread(row):
-        return jnp.broadcast_to(row, (SUB, LANE))
-
-    for cb in range(width // LANE):
-        cols = pl.ds(cb * LANE, LANE)
-        m = [spread(match[cb, q : q + 1, :]) for q in range(5)]
+        return jnp.broadcast_to(row, (SUB, WIDE))
+
+    for cb in range(width // WIDE):
+        cols = pl.ds(cb * WIDE, WIDE)
+        tile = jnp.concatenate(
+            [match[cb * (WIDE // LANE) + i] for i in range(WIDE // LANE)], axis=1
+        )
+        m = [spread(tile[q : q + 1, :]) for q in range(5)]
         visc = 0.01 * jnp.exp(0.5 * m[4])
         sigma = (0.5 * step) * m[3]
         speed = jnp.sqrt(m[1] * m[1] + m[2] * m[2] + 0.25)
@@ -189,8 +198,8 @@
             after = turned[t + 1] if t + 1 < tiles else old[t]
             grad.append((jnp.where(sub == SUB - 1, after, turned[t]) - old[t]) * inv_step)
         for sweep in range(ITERS):
-            weight_sum = jnp.zeros((SUB, LANE), jnp.float32)
-            known_sum = jnp.zeros((SUB, LANE), jnp.float32)
+            weight_sum = jnp.zeros((SUB, WIDE), jnp.float32)
+            known_sum = jnp.zeros((SUB, WIDE), jnp.float32)
             weights = []
             knowns = []
             for t in range(tiles):
@@ -211,9 +220,9 @@
             known_all = spread(jnp.sum(known_sum, axis=0, keepdims=True))
             flux = (inv_step * speed - known_all) / weight_all
             grad = [knowns[t] + flux * weights[t] for t in range(tiles)]
-        burning = lane + (first + cb * LANE) < live[0]
+        burning = lane + (first + cb * WIDE) < live_here
         burn = spread(burning.astype(jnp.int32)) > 0
-        carry = jnp.zeros((SUB, LANE), jnp.float32)
+        carry = jnp.zeros((SUB, WIDE), jnp.float32)
         for t in range(tiles):
             total = grad[t]
             for hop in (1, 2, 4):
@@ -232,7 +241,7 @@
     points, owned = profile.shape
     width = min(1024, owned)
     return pl.pallas_call(
-        functools.partial(solve_kernel, points, width),
+        functools.partial(solve_kernel, AXES, points, width),
         grid=(owned // width,),
         out_shape=(
             jax.ShapeDtypeStruct((points, owned), jnp.float32),
@@ -247,7 +256,7 @@
             pl.BlockSpec((points, width), lambda i: (0, i)),
             pl.BlockSpec((2, width), lambda i: (0, i)),
         ),
-        compiler_params=pltpu.CompilerParams(vmem_limit_bytes=32 << 20),
+        compiler_params=pltpu.CompilerParams(vmem_limit_bytes=60 << 20),
         name="wall_solve",
     )(live, profile, match)
 
@@ -297,8 +306,7 @@
     else:
         own = lax.dynamic_slice_in_dim(arrived, here % (LANE // slots) * slots, slots, axis=2)
         match = own.transpose(1, 0, 2).reshape(SUB, groups, LANE).transpose(1, 0, 2)
-    live = lax.dynamic_slice(own_live, (here,), (1,))
-    return solve(profile, match, live)
+    return solve(profile, match, own_live)
 
 
 def solution(mesh):

time: 33.6 us -> 31.9 us (0.949)
  local copies, waits for them, and re-layouts: 2.28 us -> 0 us
  Pallas kernels: 30.3 us -> 31.1 us
    dynamic_slice x1 -> x0, local copies, waits for them, and re-layouts: 1.38 us -> none  [body(): live = lax.dynamic_slice(own_live, (here,), (1,))]
    unnamed x4 -> x0, local copies, waits for them, and re-layouts: 0.9 us -> none
    pallas_call x1, Pallas kernels: 4.69 us -> 5.17 us  [solve(): pl.pallas_call(functools.partial(solve_kernel, AXES, points, width), grid...]
where the time goes in v3:
time: 31.9 us; the launch traced here: 31.7 us
  Pallas kernels  31.1 us (97%)
  between operations  0.64 us (2%)
    pallas_call x1, Pallas kernels, body(): pl.pallas_call(functools.partial(sample_kernel, AXES, (tiles_x, sections,...  25.9 us
    pallas_call x1, Pallas kernels, solve(): pl.pallas_call(functools.partial(solve_kernel, AXES, points, width), grid...  5.17 us

profile of v3, /device:TPU:0, one launch (start us, length us, event | category | flops | bytes accessed | tf_op | source)
XLA Modules:
  0.0 31.7 jit_solution(12292808910512987510)
XLA Ops:
  0.6 25.9 %sample_cells.1.match = f32[32,8,128]{2,1,0:T(8,128)} custom-call(s32[32,128]{1,0:T(8,128)} %bitcast.5, f32[5,2,128,8,128]{4,3,2,1,0:T(8,128)} %bitcast.4), custom_call_target="tpu_custom_call" | custom-call | tf_op jit(solution)/shard_map/sample_cells/pallas_call | solution.py:277
  26.5 5.2 %wall_solve.1 = (f32[64,4096]{1,0:T(8,128)}, f32[2,4096]{1,0:T(2,128)}) custom-call(s32[32]{0:T(128)} %live.1, f32[64,4096]{1,0:T(8,128)} %profile.1, f32[32,8,128]{2,1,0:T(8,128)} %sample_cells.1.match), custom_call_target="tpu_custom_call" | custom-call | tf_op jit(solution)/shard_map/wall_solve/pallas_call | solution.py:243

commit v4 on v3

--- a/solution.py
+++ b/solution.py
@@ -167,7 +167,15 @@
     pltpu.make_async_copy(every, every, send_sem).wait()
 
 
-def solve_kernel(names, points, width, live, profile, match, new_profile, wall_stress):
+def solve_kernel(
+    names, points, width, live, stored, match, solved, wall_stress, profile, new_profile, sems_in, sems_out
+):
+    chunks = [pl.ds(c * width, width) for c in range(profile.shape[1] // width)]
+    arrivals = []
+    for c, part in enumerate(chunks):
+        arrivals.append(pltpu.make_async_copy(stored.at[:, part], profile.at[:, part], sems_in.at[c]))
+        arrivals[c].start()
+    departures = []
     step = 1.0 / (points - 1)
     inv_step = float(points - 1)
     tiles = points // SUB
@@ -176,13 +184,14 @@
     index = [(sub + t * SUB).astype(jnp.float32) for t in range(tiles)]
     mixing = [0.41 * (i + 0.5) * step for i in index]
     mix_sq = [m * m for m in mixing]
-    first = pl.program_id(0) * width
     live_here = live[lax.axis_index(names[0]) * lax.axis_size(names[1]) + lax.axis_index(names[1])]
 
     def spread(row):
         return jnp.broadcast_to(row, (SUB, WIDE))
 
-    for cb in range(width // WIDE):
+    for cb in range(profile.shape[1] // WIDE):
+        if cb * WIDE % width == 0:
+            arrivals[cb * WIDE // width].wait()
         cols = pl.ds(cb * WIDE, WIDE)
         tile = jnp.concatenate(
             [match[cb * (WIDE // LANE) + i] for i in range(WIDE // LANE)], axis=1
@@ -220,7 +229,7 @@
             known_all = spread(jnp.sum(known_sum, axis=0, keepdims=True))
             flux = (inv_step * speed - known_all) / weight_all
             grad = [knowns[t] + flux * weights[t] for t in range(tiles)]
-        burning = lane + (first + cb * WIDE) < live_here
+        burning = lane + cb * WIDE < live_here
         burn = spread(burning.astype(jnp.int32)) > 0
         carry = jnp.zeros((SUB, WIDE), jnp.float32)
         for t in range(tiles):
@@ -235,27 +244,41 @@
         shear = jnp.exp(0.3 * m[0]) * visc * spread(grad[0][0:1, :])
         for row, part in enumerate((m[1], m[2])):
             wall_stress[row : row + 1, cols] = jnp.where(burn, shear * part / speed, 0.0)[0:1, :]
+        if (cb + 1) * WIDE % width == 0:
+            c = cb * WIDE // width
+            part = chunks[c]
+            departures.append(
+                pltpu.make_async_copy(new_profile.at[:, part], solved.at[:, part], sems_out.at[c])
+            )
+            departures[c].start()
+    for departure in departures:
+        departure.wait()
 
 
 def solve(profile, match, live):
     points, owned = profile.shape
-    width = min(1024, owned)
+    width = min(512, owned)
     return pl.pallas_call(
         functools.partial(solve_kernel, AXES, points, width),
-        grid=(owned // width,),
         out_shape=(
             jax.ShapeDtypeStruct((points, owned), jnp.float32),
             jax.ShapeDtypeStruct((2, owned), jnp.float32),
         ),
         in_specs=[
             pl.BlockSpec(memory_space=pltpu.SMEM),
-            pl.BlockSpec((points, width), lambda i: (0, i)),
-            pl.BlockSpec((width // LANE, SUB, LANE), lambda i: (i, 0, 0)),
+            pl.BlockSpec(memory_space=pl.ANY),
+            pl.BlockSpec(memory_space=pltpu.VMEM),
         ],
         out_specs=(
-            pl.BlockSpec((points, width), lambda i: (0, i)),
-            pl.BlockSpec((2, width), lambda i: (0, i)),
+            pl.BlockSpec(memory_space=pl.ANY),
+            pl.BlockSpec(memory_space=pltpu.VMEM),
         ),
+        scratch_shapes=[
+            pltpu.VMEM((points, owned), jnp.float32),
+            pltpu.VMEM((points, owned), jnp.float32),
+            pltpu.SemaphoreType.DMA((owned // width,)),
+            pltpu.SemaphoreType.DMA((owned // width,)),
+        ],
         compiler_params=pltpu.CompilerParams(vmem_limit_bytes=60 << 20),
         name="wall_solve",
     )(live, profile, match)

time: 31.9 us -> 33.3 us (1.044)
  Pallas kernels: 31.1 us -> 32.4 us
    pallas_call x1, Pallas kernels: 5.17 us -> 6.49 us  [solve(): pl.pallas_call(functools.partial(solve_kernel, AXES, points, width), out_...]
where the time goes in v4:
time: 33.3 us; the launch traced here: 33 us
  Pallas kernels  32.4 us (97%)
  between operations  0.64 us (2%)
    pallas_call x1, Pallas kernels, body(): pl.pallas_call(functools.partial(sample_kernel, AXES, (tiles_x, sections,...  25.9 us
    pallas_call x1, Pallas kernels, solve(): pl.pallas_call(functools.partial(solve_kernel, AXES, points, width), out_...  6.49 us

profile of v4, /device:TPU:0, one launch (start us, length us, event | category | flops | bytes accessed | tf_op | source)
XLA Modules:
  0.0 33.0 jit_solution(12970750059794720089)
XLA Ops:
  0.6 25.9 %sample_cells.1.match = f32[32,8,128]{2,1,0:T(8,128)} custom-call(s32[32,128]{1,0:T(8,128)} %bitcast.5, f32[5,2,128,8,128]{4,3,2,1,0:T(8,128)} %bitcast.4), custom_call_target="tpu_custom_call" | custom-call | tf_op jit(solution)/shard_map/sample_cells/pallas_call | solution.py:300
  26.5 6.5 %wall_solve.1 = (f32[64,4096]{1,0:T(8,128)}, f32[2,4096]{1,0:T(2,128)}) custom-call(s32[32]{0:T(128)} %live.1, f32[64,4096]{1,0:T(8,128)} %stored.1, f32[32,8,128]{2,1,0:T(8,128)} %sample_cells.1.match), custom_call_target="tpu_custom_call" | custom-call | tf_op jit(solution)/shard_map/wall_solve/pallas_call | solution.py:261
